TPU v7x, 512 devices: a whole 4x4x16 slice. The times are simulated.
512 devices in a mesh: ep: 128 (over z, y, core), dp: 4 (over x).
Axes of the slice: x: 4, y: 4, z: 16, core: 2. Of those that a mesh axis runs over, the one named last changes fastest.
Arguments:
- out_grads: bfloat16 [65536, 2048], P(('ep', 'dp')), may hold values from -40 to 40
- hidden_acts: bfloat16 [65536, 512], P(('ep', 'dp')), may hold values from -20 to 20
- routing: int32 [65536, 1], P(('ep', 'dp')), may hold values from 0 to 95, as said below
- replica_pick: int32 [65536], P(('ep', 'dp')), may hold values from 0 to 3
- master_weights: float32 [128, 2048, 512], P('ep', 'dp'), may hold values from -0.25 to 0.25
- current_slots: int32 [128], replicated, may hold values from 0 to 95, as said below
- next_slots: int32 [128], replicated, may hold values from 0 to 95, as said below
Outputs:
- input_grads: float32 [65536, 512], P(('ep', 'dp'))
- moved_weights: float32 [128, 2048, 512], P('ep', 'dp')
- moved_updates: float32 [128, 2048, 512], P('ep', 'dp')
Inputs may be any that keep to these rules, and one draw needn't show every extreme that they name: `routing`: the rows of one device name each expert at most 2 times; the experts held by two slots now are named exactly 2 times by the rows of every device. `current_slots`: every expert below 96 is held by one or two slots. `next_slots`: every expert below 96 is held by at least one slot.
All inputs are finite; a program needn't handle non-finite values.
Results may differ from a plain program's by a relative error of at most 0.0029.
Values may be sent and summed in bfloat16 or wider, within the bound.
A program may use at most 64 MiB of HBM per device.

v0:
```python
import jax
import jax.numpy as jnp
from jax import lax
from jax.sharding import PartitionSpec as P

D = 2048
NS_STEPS = 2
POLY_FIRST = 3.4445
POLY_SECOND = -4.775
POLY_THIRD = 2.0315
LEARNING_RATE = 0.02
UPDATE_SCALE = 0.2
EPSILON = 1e-07
PRECISE = lax.Precision.HIGHEST


def slot_ranks(placement):
    number = placement.shape[0]
    matching = placement[:, None] == placement[None, :]
    earlier = (
        jnp.arange(number, dtype=jnp.int32)[None, :] < jnp.arange(number, dtype=jnp.int32)[:, None]
    )
    return jnp.sum(matching & earlier, axis=1)


def choose_slots(placement, rankings, experts_named, wanted_index):
    holders = placement[None, :] == experts_named[:, None]
    totals = jnp.sum(holders, axis=1)
    wanted = jnp.remainder(wanted_index, totals)
    chosen = holders & (rankings[None, :] == wanted[:, None])
    ordinal = jnp.arange(placement.shape[0], dtype=jnp.int32)[None, :]
    return jnp.sum(jnp.where(chosen, ordinal, 0), axis=1)


def gram_of(matrix):
    return lax.dot_general(matrix, matrix, (((0,), (0,)), ((), ())), precision=PRECISE)


def orthogonalize(grad):
    squares = lax.psum(jnp.sum(grad * grad), "dp")
    normed = grad / (jnp.sqrt(squares) + EPSILON)
    gram_now = lax.psum(gram_of(normed), "dp")
    for iteration in range(NS_STEPS):
        if iteration > 0:
            gram_now = lax.psum(gram_of(normed), "dp")
        polynomial = POLY_SECOND * gram_now + POLY_THIRD * jnp.dot(
            gram_now, gram_now, precision=PRECISE
        )
        normed = POLY_FIRST * normed + jnp.dot(normed, polynomial, precision=PRECISE)
    return UPDATE_SCALE * D**0.5 * normed


def per_device(
    out_grads, hidden_acts, routing, replica_pick, master_weights, current_slots, next_slots
):
    tok_rows = out_grads.shape[0]
    model_width = out_grads.shape[1]
    expert_width = hidden_acts.shape[1]
    ep_size = lax.axis_size("ep")
    capacity = 2 * tok_rows // ep_size
    local_master = master_weights[0]
    rankings = slot_ranks(current_slots)
    slot_of_row = choose_slots(current_slots, rankings, routing[:, 0], replica_pick)
    onehot_slots = (slot_of_row[:, None] == jnp.arange(ep_size, dtype=jnp.int32)[None, :]).astype(
        jnp.int32
    )
    running = jnp.cumsum(onehot_slots, axis=0)
    position = jnp.sum(onehot_slots * (running - 1), axis=1)
    target = slot_of_row * capacity + position
    send_grads = (
        jnp.zeros((ep_size * capacity, model_width), jnp.bfloat16).at[target].set(out_grads)
    )
    send_acts = (
        jnp.zeros((ep_size * capacity, expert_width), jnp.bfloat16).at[target].set(hidden_acts)
    )
    recv_grads, recv_acts = (
        lax.all_to_all(
            send_grads.reshape(ep_size, capacity, model_width),
            "ep",
            split_axis=0,
            concat_axis=0,
            tiled=True,
        ),
        lax.all_to_all(
            send_acts.reshape(ep_size, capacity, expert_width),
            "ep",
            split_axis=0,
            concat_axis=0,
            tiled=True,
        ),
    )
    rows_grads = recv_grads.reshape(-1, model_width)
    rows_acts = recv_acts.reshape(-1, expert_width)
    weight_copy = local_master.astype(jnp.bfloat16)
    columns = rows_grads
    gathered = jnp.dot(
        columns,
        lax.all_gather(weight_copy, "dp", axis=0, tiled=True),
        preferred_element_type=jnp.float32,
    )
    returned = lax.all_to_all(
        gathered.reshape(ep_size, capacity, expert_width),
        "ep",
        split_axis=0,
        concat_axis=0,
        tiled=True,
    )
    input_grads = returned.reshape(-1, expert_width)[target]
    columns = rows_grads
    slot_grad = lax.psum_scatter(
        lax.dot_general(
            columns, rows_acts, (((0,), (0,)), ((), ())), preferred_element_type=jnp.float32
        ),
        "dp",
        scatter_dimension=0,
        tiled=True,
    )
    piece_len = local_master.shape[0] * local_master.shape[1] // ep_size
    homes_next = choose_slots(current_slots, rankings, next_slots, jnp.zeros_like(next_slots))
    matching = (current_slots[:, None] == current_slots[None, :]).astype(jnp.float32)
    spread = lax.all_to_all(
        slot_grad.reshape(ep_size, piece_len), "ep", split_axis=0, concat_axis=0, tiled=True
    )
    summed = jnp.dot(matching, spread, precision=PRECISE)
    expert_grad = lax.all_to_all(summed, "ep", split_axis=0, concat_axis=0, tiled=True).reshape(
        local_master.shape
    )
    update = orthogonalize(expert_grad)
    fresh = local_master - LEARNING_RATE * update
    pieces_weight, pieces_update = (
        lax.all_to_all(
            fresh.reshape(ep_size, piece_len), "ep", split_axis=0, concat_axis=0, tiled=True
        ),
        lax.all_to_all(
            update.reshape(ep_size, piece_len), "ep", split_axis=0, concat_axis=0, tiled=True
        ),
    )
    chosen_weight = jnp.take(pieces_weight, homes_next, axis=0)
    chosen_update = jnp.take(pieces_update, homes_next, axis=0)
    arrived_weight, arrived_update = (
        lax.all_to_all(chosen_weight, "ep", split_axis=0, concat_axis=0, tiled=True),
        lax.all_to_all(chosen_update, "ep", split_axis=0, concat_axis=0, tiled=True),
    )
    moved_weight = arrived_weight.reshape(local_master.shape)
    moved_update = arrived_update.reshape(local_master.shape)
    return (input_grads, moved_weight[None], moved_update[None])


def solution(mesh):
    placed = (
        P(("ep", "dp"), None),
        P(("ep", "dp"), None),
        P(("ep", "dp"), None),
        P(("ep", "dp")),
        P("ep", "dp", None),
        P(),
        P(),
    )
    return jax.shard_map(
        per_device,
        mesh=mesh,
        in_specs=placed,
        out_specs=(P(("ep", "dp"), None), P("ep", "dp", None), P("ep", "dp", None)),
        check_vma=False,
    )
```

profile of v0, /device:TPU:33, one launch (start us, length us, event | category | flops | bytes accessed | tf_op | source)
XLA Modules:
  0.0 765.5 jit_solution(6440641814367399283)
XLA Ops:
  14.0 19.5 %all-to-all-start = ((bf16[128,2,2048]{2,1,0:T(2,128)(2,1)}), bf16[128,2,2048]{2,1,0:T(2,128)(2,1)S(1)}, u32[]{:S(2)}, u32[]{:S(2)}) async-start(bf16[128,2,2048]{2,1,0:T(2,128)(2,1)} %reshape.99), calls=%async_computation | async-start | bytes 2097152 | tf_op jit(solution)/shard_map/all_to_all | solution.py:77
  35.8 53.3 %all-to-all-done = bf16[128,2,2048]{2,1,0:T(2,128)(2,1)S(1)} async-done(((bf16[128,2,2048]{2,1,0:T(2,128)(2,1)}), bf16[128,2,2048]{2,1,0:T(2,128)(2,1)S(1)}, u32[]{:S(2)}, u32[]{:S(2)}) %all-to-all-start) | async-done | bytes 1048608 | tf_op jit(solution)/shard_map/all_to_all | solution.py:77
  89.1 6.4 all-to-all-start.2
  96.6 21.5 %all-to-all-done.2 = bf16[128,2,512]{2,1,0:T(2,128)(2,1)S(1)} async-done(((bf16[128,2,512]{2,1,0:T(2,128)(2,1)}), bf16[128,2,512]{2,1,0:T(2,128)(2,1)S(1)}, u32[]{:S(2)}, u32[]{:S(2)}) %all-to-all-start.2) | async-done | bytes 262176 | tf_op jit(solution)/shard_map/all_to_all | solution.py:84
  120.8 45.4 %reduce-scatter.2.cloned.1.call-done = f32[512,512]{1,0:T(8,128)} async-done(((f32[2048,512]{1,0:T(8,128)}), f32[512,512]{1,0:T(8,128)}) %reduce-scatter.2.cloned.1.call-update) | async-done | bytes 1048592 | tf_op jit(solution)/shard_map/reduce_scatter | solution.py:110
  168.8 72.3 %all_to_all.81 = f32[128,1,2048]{2,1,0:T(1,128)S(1)} all-to-all(f32[128,1,2048]{2,1,0:T(1,128)S(1)} %all_to_all.69), channel_id=1, replica_groups=mesh['ep'=128,'dp'=4] {'ep'}, dimensions={0} | all-to-all | bytes 2097152 | tf_op jit(solution)/shard_map/all_to_all | solution.py:121
  243.1 61.9 %all_to_all.82 = f32[128,1,2048]{2,1,0:T(1,128)S(1)} all-to-all(f32[128,1,2048]{2,1,0:T(1,128)S(1)} %copy.20), channel_id=1, replica_groups=mesh['ep'=128,'dp'=4] {'ep'}, dimensions={0} | all-to-all | bytes 2097152 | tf_op jit(solution)/shard_map/all_to_all | solution.py:125
  307.7 7.2 psum.21
  321.7 50.9 %all-reduce.3.cloned.1.call-done = f32[512,512]{1,0:T(8,128)} async-done(((f32[512,512]{1,0:T(8,128)}), f32[512,512]{1,0:T(8,128)}) %all-reduce.3.cloned.1.call-update) | async-done | bytes 1048592 | tf_op jit(solution)/shard_map/psum | solution.py:42
  372.6 3.9 fusion.3
  381.2 62.3 %all-reduce.5.cloned.1.call-done = f32[512,512]{1,0:T(8,128)} async-done(((f32[512,512]{1,0:T(8,128)}), f32[512,512]{1,0:T(8,128)}) %all-reduce.5.cloned.1.call-update) | async-done | bytes 1048592 | tf_op jit(solution)/shard_map/psum | solution.py:45
  443.5 3.9 fusion.2
  450.8 3.6 all_to_all.71
  454.3 18.6 %all-to-all-start.7 = ((f32[128,1,2048]{2,1,0:T(1,128)}), f32[128,1,2048]{2,1,0:T(1,128)}, u32[]{:S(2)}, u32[]{:S(2)}) async-start(f32[128,1,2048]{2,1,0:T(1,128)} %all_to_all.71), calls=%async_computation.8 | async-start | bytes 2097152 | tf_op jit(solution)/shard_map/all_to_all | solution.py:134
  475.2 53.0 %all-to-all-done.7 = f32[128,1,2048]{2,1,0:T(1,128)} async-done(((f32[128,1,2048]{2,1,0:T(1,128)}), f32[128,1,2048]{2,1,0:T(1,128)}, u32[]{:S(2)}, u32[]{:S(2)}) %all-to-all-start.7) | async-done | bytes 1048608 | tf_op jit(solution)/shard_map/all_to_all | solution.py:134
  528.2 6.4 all-to-all-start.5
  535.6 41.3 %all-gather.2.cloned.1.call-done = bf16[2048,512]{1,0:T(8,128)(2,1)} async-done(((bf16[512,512]{1,0:T(8,128)(2,1)}), bf16[2048,512]{1,0:T(8,128)(2,1)}) %all-gather.2.cloned.1.call-update) | async-done | bytes 2097168 | tf_op jit(solution)/shard_map/all_gather | solution.py:98
  580.4 9.9 %all-to-all-done.5 = f32[128,1,2048]{2,1,0:T(1,128)S(1)} async-done(((f32[128,1,2048]{2,1,0:T(1,128)}), f32[128,1,2048]{2,1,0:T(1,128)S(1)}, u32[]{:S(2)}, u32[]{:S(2)}) %all-to-all-start.5) | async-done | bytes 1048608 | tf_op jit(solution)/shard_map/all_to_all | solution.py:131
  590.3 7.3 all-to-all-start.1
  603.8 27.0 %all-to-all-done.1 = f32[128,2,512]{2,1,0:T(2,128)} async-done(((f32[128,2,512]{2,1,0:T(2,128)}), f32[128,2,512]{2,1,0:T(2,128)}, u32[]{:S(2)}, u32[]{:S(2)}) %all-to-all-start.1) | async-done | bytes 524320 | tf_op jit(solution)/shard_map/all_to_all | solution.py:101
  630.9 6.6 all-to-all-start.6
  639.6 53.4 %all-to-all-done.6 = f32[128,1,2048]{2,1,0:T(1,128)S(1)} async-done(((f32[128,1,2048]{2,1,0:T(1,128)}), f32[128,1,2048]{2,1,0:T(1,128)S(1)}, u32[]{:S(2)}, u32[]{:S(2)}) %all-to-all-start.6) | async-done | bytes 1048608 | tf_op jit(solution)/shard_map/all_to_all | solution.py:141
  693.0 6.4 all-to-all-start.8
  706.1 49.0 %all-to-all-done.8 = f32[128,1,2048]{2,1,0:T(1,128)S(1)} async-done(((f32[128,1,2048]{2,1,0:T(1,128)}), f32[128,1,2048]{2,1,0:T(1,128)S(1)}, u32[]{:S(2)}, u32[]{:S(2)}) %all-to-all-start.8) | async-done | bytes 1048608 | tf_op jit(solution)/shard_map/all_to_all | solution.py:142
  (58 shorter events, 59.4 us)
Async XLA Ops:
  14.0 75.1 %all-to-all-start = ((bf16[128,2,2048]{2,1,0:T(2,128)(2,1)}), bf16[128,2,2048]{2,1,0:T(2,128)(2,1)S(1)}, u32[]{:S(2)}, u32[]{:S(2)}) async-start(bf16[128,2,2048]{2,1,0:T(2,128)(2,1)} %reshape.99), calls=%async_computation | async-start | bytes 2097152 | tf_op jit(solution)/shard_map/all_to_all | solution.py:77
  89.1 29.0 %all-to-all-start.2 = ((bf16[128,2,512]{2,1,0:T(2,128)(2,1)}), bf16[128,2,512]{2,1,0:T(2,128)(2,1)S(1)}, u32[]{:S(2)}, u32[]{:S(2)}) async-start(bf16[128,2,512]{2,1,0:T(2,128)(2,1)} %reshape.101), calls=%async_computation.2 | async-start | bytes 524288 | tf_op jit(solution)/shard_map/all_to_all | solution.py:84
  95.6 70.7 %reduce-scatter.2.cloned.1.call-start = ((), (), s32[]{:S(2)}) async-start(), calls=%async_computation.11 | async-start | bytes 5242880 | tf_op jit(solution)/shard_map/reduce_scatter | solution.py:110
  120.8 120.3 %copy-start.2 = (s32[128]{0:T(128)S(1)}, s32[128]{0:T(128)}, u32[]{:S(2)}) copy-start(s32[128]{0:T(128)} %param.14) | copy-start | bytes 1540
  120.8 251.8 %all-reduce.3.cloned.1.call-start = ((), (), s32[]{:S(2)}) async-start(), calls=%async_computation.12 | async-start | bytes 2097152 | tf_op jit(solution)/shard_map/psum | solution.py:42
  321.4 122.1 %all-reduce.5.cloned.1.call-start = ((), (), s32[]{:S(2)}) async-start(), calls=%async_computation.13 | async-start | bytes 2097152 | tf_op jit(solution)/shard_map/psum | solution.py:45
  381.2 66.3 %copy-start = (f32[1,512,512]{2,1,0:T(8,128)S(1)}, f32[1,512,512]{2,1,0:T(8,128)}, u32[]{:S(2)}) copy-start(f32[1,512,512]{2,1,0:T(8,128)} %param.13) | copy-start | bytes 3145732
  450.8 22.2 %copy-start.1 = (f32[512,512]{1,0:T(8,128)S(1)}, f32[512,512]{1,0:T(8,128)}, u32[]{:S(2)}) copy-start(f32[512,512]{1,0:T(8,128)} %get-tuple-element.10) | copy-start | bytes 3145732
  454.3 73.9 %all-to-all-start.7 = ((f32[128,1,2048]{2,1,0:T(1,128)}), f32[128,1,2048]{2,1,0:T(1,128)}, u32[]{:S(2)}, u32[]{:S(2)}) async-start(f32[128,1,2048]{2,1,0:T(1,128)} %all_to_all.71), calls=%async_computation.8 | async-start | bytes 2097152 | tf_op jit(solution)/shard_map/all_to_all | solution.py:134
  528.2 62.1 %all-to-all-start.5 = ((f32[128,1,2048]{2,1,0:T(1,128)}), f32[128,1,2048]{2,1,0:T(1,128)S(1)}, u32[]{:S(2)}, u32[]{:S(2)}) async-start(f32[128,1,2048]{2,1,0:T(1,128)} %all_to_all.70), calls=%async_computation.6 | async-start | bytes 2097152 | tf_op jit(solution)/shard_map/all_to_all | solution.py:131
  534.7 42.2 %all-gather.2.cloned.1.call-start = ((), (), s32[]{:S(2)}) async-start(), calls=%async_computation.10 | async-start | bytes 2621440 | tf_op jit(solution)/shard_map/all_gather | solution.py:98
  590.3 40.6 %all-to-all-start.1 = ((f32[128,2,512]{2,1,0:T(2,128)}), f32[128,2,512]{2,1,0:T(2,128)}, u32[]{:S(2)}, u32[]{:S(2)}) async-start(f32[128,2,512]{2,1,0:T(2,128)} %copy.16), calls=%async_computation.1 | async-start | bytes 1048576 | tf_op jit(solution)/shard_map/all_to_all | solution.py:101
  630.9 62.1 %all-to-all-start.6 = ((f32[128,1,2048]{2,1,0:T(1,128)}), f32[128,1,2048]{2,1,0:T(1,128)S(1)}, u32[]{:S(2)}, u32[]{:S(2)}) async-start(f32[128,1,2048]{2,1,0:T(1,128)} %copy.22), calls=%async_computation.7 | async-start | bytes 2097152 | tf_op jit(solution)/shard_map/all_to_all | solution.py:141
  693.0 62.1 %all-to-all-start.8 = ((f32[128,1,2048]{2,1,0:T(1,128)}), f32[128,1,2048]{2,1,0:T(1,128)S(1)}, u32[]{:S(2)}, u32[]{:S(2)}) async-start(f32[128,1,2048]{2,1,0:T(1,128)} %copy.24), calls=%async_computation.9 | async-start | bytes 2097152 | tf_op jit(solution)/shard_map/all_to_all | solution.py:142
Sparse Core Ops, SparseCore 0:
  120.9 45.3 reduce-scatter.1
  321.5 51.0 all-reduce.2
  381.3 62.1 all-reduce.4
  538.1 38.7 all-gather.1
where the time goes:
time: 774 us; the launch traced here: 766 us
  waiting for transfers between devices  467 us (60%)
  blocking collectives  141 us (18%)
  starting transfers between devices  71.7 us (9%)
  local copies, waits for them, and re-layouts  31.3 us (4%)
  matrix products  24.6 us (3%)
  between operations  14.9 us (2%)
  other arithmetic  14.6 us (2%)
    psum x2, waiting for transfers between devices, orthogonalize(): gram_now = lax.psum(gram_of(normed), 'dp')  113 us
    all_to_all x1, blocking collectives, per_device(): lax.all_to_all(slot_grad.reshape(ep_size, piece_len), 'ep', split_axis=0,...  72.3 us
    all_to_all x1, blocking collectives, per_device(): lax.all_to_all(summed, 'ep', split_axis=0, concat_axis=0, tiled=True)  61.9 us
    all_to_all x1, waiting for transfers between devices, per_device(): lax.all_to_all(chosen_weight, 'ep', split_axis=0, concat_axis=0, tiled=True)  53.4 us
    all_to_all x1, waiting for transfers between devices, per_device(): lax.all_to_all(send_grads.reshape(ep_size, capacity, model_width), 'ep',...  53.3 us
    all_to_all x1, waiting for transfers between devices, per_device(): lax.all_to_all(update.reshape(ep_size, piece_len), 'ep', split_axis=0, co...  53 us
    all_to_all x1, waiting for transfers between devices, per_device(): lax.all_to_all(chosen_update, 'ep', split_axis=0, concat_axis=0, tiled=True)  49 us
    reduce_scatter x1, waiting for transfers between devices, per_device(): lax.psum_scatter(lax.dot_general(columns, rows_acts, (((0,), (0,)), ((),...  45.4 us
  transfers between devices with their start and end apart: 11, of which 11 were waited for; matrix products, arithmetic and copies ran while one was open for 3% of the time, Pallas kernels for 0%

commit v1 on v0

--- a/solution.py
+++ b/solution.py
@@ -12,6 +12,22 @@
 UPDATE_SCALE = 0.2
 EPSILON = 1e-07
 PRECISE = lax.Precision.HIGHEST
+
+
+def gather_around(x, axis, dim):
+    ways, here, hop = (lax.axis_size(axis), lax.axis_index(axis), x.shape[dim])
+    shape = [n * ways if d == dim else n for d, n in enumerate(x.shape)]
+    full = lax.dynamic_update_slice_in_dim(jnp.zeros(shape, x.dtype), x, here * hop, axis=dim)
+    going_up = going_down = x
+    for far in range(1, ways // 2 + 1):
+        going_up = lax.ppermute(going_up, axis, [(d, (d + 1) % ways) for d in range(ways)])
+        full = lax.dynamic_update_slice_in_dim(full, going_up, (here - far) % ways * hop, axis=dim)
+        if 2 * far < ways:
+            going_down = lax.ppermute(going_down, axis, [(d, (d - 1) % ways) for d in range(ways)])
+            full = lax.dynamic_update_slice_in_dim(
+                full, going_down, (here + far) % ways * hop, axis=dim
+            )
+    return full
 
 
 def slot_ranks(placement):
@@ -94,9 +110,7 @@
     weight_copy = local_master.astype(jnp.bfloat16)
     columns = rows_grads
     gathered = jnp.dot(
-        columns,
-        lax.all_gather(weight_copy, "dp", axis=0, tiled=True),
-        preferred_element_type=jnp.float32,
+        columns, gather_around(weight_copy, "dp", 0), preferred_element_type=jnp.float32
     )
     returned = lax.all_to_all(
         gathered.reshape(ep_size, capacity, expert_width),

time: 774 us -> 774 us (level)
  waiting for transfers between devices: 467 us -> 456 us
    all_gather x1 -> x0, waiting for transfers between devices: 41.3 us -> none  [per_device(): lax.all_gather(weight_copy, 'dp', axis=0, tiled=True)]
    ppermute x0 -> x3, waiting for transfers between devices: none -> 21.5 us  [the longest x2 21.5 us: gather_around(): lax.ppermute(going_up, axis, [(d, (d + 1) % ways) for d in range(ways)])]
    ppermute x0 -> x3, starting transfers between devices: none -> 8.39 us  [the longest x2 4.21 us: gather_around(): lax.ppermute(going_up, axis, [(d, (d + 1) % ways) for d in range(ways)])]
    all_to_all x1, waiting for transfers between devices: 9.87 us -> 17.7 us  [per_device(): lax.all_to_all(fresh.reshape(ep_size, piece_len), 'ep', split_axis=0, con...]
  transfers between devices with their start and end apart: 11 -> 13, of which waited for: 11 -> 12; matrix products, arithmetic and copies ran while one was open for 3% -> 3% of each run, Pallas kernels for 0% -> 0%
where the time goes in v1:
time: 774 us; the launch traced here: 765 us
  waiting for transfers between devices  456 us (59%)
  blocking collectives  141 us (18%)
  starting transfers between devices  79.4 us (10%)
  local copies, waits for them, and re-layouts  34.7 us (4%)
  matrix products  23 us (3%)
  other arithmetic  15.8 us (2%)
  between operations  15 us (2%)
    psum x2, waiting for transfers between devices, orthogonalize(): gram_now = lax.psum(gram_of(normed), 'dp')  113 us
    all_to_all x1, blocking collectives, per_device(): lax.all_to_all(slot_grad.reshape(ep_size, piece_len), 'ep', split_axis=0,...  72.3 us
    all_to_all x1, blocking collectives, per_device(): lax.all_to_all(summed, 'ep', split_axis=0, concat_axis=0, tiled=True)  61.9 us
    all_to_all x1, waiting for transfers between devices, per_device(): lax.all_to_all(chosen_weight, 'ep', split_axis=0, concat_axis=0, tiled=True)  53.5 us
    all_to_all x1, waiting for transfers between devices, per_device(): lax.all_to_all(update.reshape(ep_size, piece_len), 'ep', split_axis=0, co...  53.4 us
    all_to_all x1, waiting for transfers between devices, per_device(): lax.all_to_all(send_grads.reshape(ep_size, capacity, model_width), 'ep',...  53.3 us
    all_to_all x1, waiting for transfers between devices, per_device(): lax.all_to_all(chosen_update, 'ep', split_axis=0, concat_axis=0, tiled=True)  49 us
    reduce_scatter x1, waiting for transfers between devices, per_device(): lax.psum_scatter(lax.dot_general(columns, rows_acts, (((0,), (0,)), ((),...  45.4 us
  transfers between devices with their start and end apart: 13, of which 12 were waited for; matrix products, arithmetic and copies ran while one was open for 3% of the time, Pallas kernels for 0%

profile of v1, /device:TPU:33, one launch (start us, length us, event | category | flops | bytes accessed | tf_op | source)
XLA Modules:
  0.0 764.9 jit_solution(14195670401971763281)
XLA Ops:
  14.0 19.5 %all-to-all-start = ((bf16[128,2,2048]{2,1,0:T(2,128)(2,1)}), bf16[128,2,2048]{2,1,0:T(2,128)(2,1)S(1)}, u32[]{:S(2)}, u32[]{:S(2)}) async-start(bf16[128,2,2048]{2,1,0:T(2,128)(2,1)} %reshape.99), calls=%async_computation | async-start | bytes 2097152 | tf_op jit(solution)/shard_map/all_to_all | solution.py:93
  35.8 53.3 %all-to-all-done = bf16[128,2,2048]{2,1,0:T(2,128)(2,1)S(1)} async-done(((bf16[128,2,2048]{2,1,0:T(2,128)(2,1)}), bf16[128,2,2048]{2,1,0:T(2,128)(2,1)S(1)}, u32[]{:S(2)}, u32[]{:S(2)}) %all-to-all-start) | async-done | bytes 1048608 | tf_op jit(solution)/shard_map/all_to_all | solution.py:93
  89.1 6.4 all-to-all-start.2
  96.6 21.5 %all-to-all-done.2 = bf16[128,2,512]{2,1,0:T(2,128)(2,1)S(1)} async-done(((bf16[128,2,512]{2,1,0:T(2,128)(2,1)}), bf16[128,2,512]{2,1,0:T(2,128)(2,1)S(1)}, u32[]{:S(2)}, u32[]{:S(2)}) %all-to-all-start.2) | async-done | bytes 262176 | tf_op jit(solution)/shard_map/all_to_all | solution.py:100
  120.8 45.4 %reduce-scatter.2.cloned.1.call-done = f32[512,512]{1,0:T(8,128)} async-done(((f32[2048,512]{1,0:T(8,128)}), f32[512,512]{1,0:T(8,128)}) %reduce-scatter.2.cloned.1.call-update) | async-done | bytes 1048592 | tf_op jit(solution)/shard_map/reduce_scatter | solution.py:124
  168.8 72.3 %all_to_all.81 = f32[128,1,2048]{2,1,0:T(1,128)S(1)} all-to-all(f32[128,1,2048]{2,1,0:T(1,128)S(1)} %all_to_all.69), channel_id=1, replica_groups=mesh['ep'=128,'dp'=4] {'ep'}, dimensions={0} | all-to-all | bytes 2097152 | tf_op jit(solution)/shard_map/all_to_all | solution.py:135
  243.1 61.9 %all_to_all.82 = f32[128,1,2048]{2,1,0:T(1,128)S(1)} all-to-all(f32[128,1,2048]{2,1,0:T(1,128)S(1)} %copy.20), channel_id=1, replica_groups=mesh['ep'=128,'dp'=4] {'ep'}, dimensions={0} | all-to-all | bytes 2097152 | tf_op jit(solution)/shard_map/all_to_all | solution.py:139
  307.7 7.2 psum.21
  321.7 50.9 %all-reduce.3.cloned.1.call-done = f32[512,512]{1,0:T(8,128)} async-done(((f32[512,512]{1,0:T(8,128)}), f32[512,512]{1,0:T(8,128)}) %all-reduce.3.cloned.1.call-update) | async-done | bytes 1048592 | tf_op jit(solution)/shard_map/psum | solution.py:58
  381.2 62.3 %all-reduce.5.cloned.1.call-done = f32[512,512]{1,0:T(8,128)} async-done(((f32[512,512]{1,0:T(8,128)}), f32[512,512]{1,0:T(8,128)}) %all-reduce.5.cloned.1.call-update) | async-done | bytes 1048592 | tf_op jit(solution)/shard_map/psum | solution.py:61
  443.5 3.9 fusion.2
  454.3 18.1 %all-to-all-start.7 = ((f32[128,1,2048]{2,1,0:T(1,128)}), f32[128,1,2048]{2,1,0:T(1,128)S(1)}, u32[]{:S(2)}, u32[]{:S(2)}) async-start(f32[128,1,2048]{2,1,0:T(1,128)} %all_to_all.71), calls=%async_computation.8 | async-start | bytes 2097152 | tf_op jit(solution)/shard_map/all_to_all | solution.py:148
  474.7 53.4 %all-to-all-done.7 = f32[128,1,2048]{2,1,0:T(1,128)S(1)} async-done(((f32[128,1,2048]{2,1,0:T(1,128)}), f32[128,1,2048]{2,1,0:T(1,128)S(1)}, u32[]{:S(2)}, u32[]{:S(2)}) %all-to-all-start.7) | async-done | bytes 1048608 | tf_op jit(solution)/shard_map/all_to_all | solution.py:148
  528.1 6.9 all-to-all-start.5
  539.6 4.2 collective-permute-start.1
  543.8 10.1 %collective-permute-done = bf16[512,512]{1,0:T(8,128)(2,1)} collective-permute-done((bf16[512,512]{1,0:T(8,128)(2,1)}, bf16[512,512]{1,0:T(8,128)(2,1)}, u32[]{:S(2)}, u32[]{:S(2)}) %collective-permute-start) | collective-permute-done | bytes 524320 | tf_op jit(solution)/shard_map/ppermute | solution.py:23
  558.0 11.5 %collective-permute-done.2 = bf16[512,512]{1,0:T(8,128)(2,1)} collective-permute-done((bf16[512,512]{1,0:T(8,128)(2,1)}, bf16[512,512]{1,0:T(8,128)(2,1)}, u32[]{:S(2)}, u32[]{:S(2)}) %collective-permute-start.2) | collective-permute-done | bytes 524320 | tf_op jit(solution)/shard_map/ppermute | solution.py:23
  572.5 17.7 %all-to-all-done.5 = f32[128,1,2048]{2,1,0:T(1,128)} async-done(((f32[128,1,2048]{2,1,0:T(1,128)}), f32[128,1,2048]{2,1,0:T(1,128)}, u32[]{:S(2)}, u32[]{:S(2)}) %all-to-all-start.5) | async-done | bytes 1048608 | tf_op jit(solution)/shard_map/all_to_all | solution.py:145
  590.3 6.9 all-to-all-start.1
  603.4 27.0 %all-to-all-done.1 = f32[128,2,512]{2,1,0:T(2,128)} async-done(((f32[128,2,512]{2,1,0:T(2,128)}), f32[128,2,512]{2,1,0:T(2,128)}, u32[]{:S(2)}, u32[]{:S(2)}) %all-to-all-start.1) | async-done | bytes 524320 | tf_op jit(solution)/shard_map/all_to_all | solution.py:115
  630.4 6.3 all-to-all-start.6
  638.8 53.5 %all-to-all-done.6 = f32[128,1,2048]{2,1,0:T(1,128)S(1)} async-done(((f32[128,1,2048]{2,1,0:T(1,128)}), f32[128,1,2048]{2,1,0:T(1,128)S(1)}, u32[]{:S(2)}, u32[]{:S(2)}) %all-to-all-start.6) | async-done | bytes 1048608 | tf_op jit(solution)/shard_map/all_to_all | solution.py:155
  692.4 6.4 all-to-all-start.8
  705.4 49.0 %all-to-all-done.8 = f32[128,1,2048]{2,1,0:T(1,128)S(1)} async-done(((f32[128,1,2048]{2,1,0:T(1,128)}), f32[128,1,2048]{2,1,0:T(1,128)S(1)}, u32[]{:S(2)}, u32[]{:S(2)}) %all-to-all-start.8) | async-done | bytes 1048608 | tf_op jit(solution)/shard_map/all_to_all | solution.py:156
  (69 shorter events, 74.1 us)
Async XLA Ops:
  14.0 75.1 %all-to-all-start = ((bf16[128,2,2048]{2,1,0:T(2,128)(2,1)}), bf16[128,2,2048]{2,1,0:T(2,128)(2,1)S(1)}, u32[]{:S(2)}, u32[]{:S(2)}) async-start(bf16[128,2,2048]{2,1,0:T(2,128)(2,1)} %reshape.99), calls=%async_computation | async-start | bytes 2097152 | tf_op jit(solution)/shard_map/all_to_all | solution.py:93
  89.1 29.0 %all-to-all-start.2 = ((bf16[128,2,512]{2,1,0:T(2,128)(2,1)}), bf16[128,2,512]{2,1,0:T(2,128)(2,1)S(1)}, u32[]{:S(2)}, u32[]{:S(2)}) async-start(bf16[128,2,512]{2,1,0:T(2,128)(2,1)} %reshape.101), calls=%async_computation.2 | async-start | bytes 524288 | tf_op jit(solution)/shard_map/all_to_all | solution.py:100
  95.6 70.7 %reduce-scatter.2.cloned.1.call-start = ((), (), s32[]{:S(2)}) async-start(), calls=%async_computation.10 | async-start | bytes 5242880 | tf_op jit(solution)/shard_map/reduce_scatter | solution.py:124
  120.8 120.3 %copy-start.4 = (s32[128]{0:T(128)S(1)}, s32[128]{0:T(128)}, u32[]{:S(2)}) copy-start(s32[128]{0:T(128)} %param.14) | copy-start | bytes 1540
  120.8 251.8 %all-reduce.3.cloned.1.call-start = ((), (), s32[]{:S(2)}) async-start(), calls=%async_computation.11 | async-start | bytes 2097152 | tf_op jit(solution)/shard_map/psum | solution.py:58
  321.4 122.1 %all-reduce.5.cloned.1.call-start = ((), (), s32[]{:S(2)}) async-start(), calls=%async_computation.12 | async-start | bytes 2097152 | tf_op jit(solution)/shard_map/psum | solution.py:61
  381.2 66.3 %copy-start = (f32[1,512,512]{2,1,0:T(8,128)S(1)}, f32[1,512,512]{2,1,0:T(8,128)}, u32[]{:S(2)}) copy-start(f32[1,512,512]{2,1,0:T(8,128)} %param.13) | copy-start | bytes 3145732
  450.8 21.7 %copy-start.1 = (f32[512,512]{1,0:T(8,128)S(1)}, f32[512,512]{1,0:T(8,128)}, u32[]{:S(2)}) copy-start(f32[512,512]{1,0:T(8,128)} %get-tuple-element.12) | copy-start | bytes 3145732
  454.3 73.8 %all-to-all-start.7 = ((f32[128,1,2048]{2,1,0:T(1,128)}), f32[128,1,2048]{2,1,0:T(1,128)S(1)}, u32[]{:S(2)}, u32[]{:S(2)}) async-start(f32[128,1,2048]{2,1,0:T(1,128)} %all_to_all.71), calls=%async_computation.8 | async-start | bytes 2097152 | tf_op jit(solution)/shard_map/all_to_all | solution.py:148
  528.1 6.9 copy-start.2
  528.1 62.2 %all-to-all-start.5 = ((f32[128,1,2048]{2,1,0:T(1,128)}), f32[128,1,2048]{2,1,0:T(1,128)}, u32[]{:S(2)}, u32[]{:S(2)}) async-start(f32[128,1,2048]{2,1,0:T(1,128)} %all_to_all.70), calls=%async_computation.6 | async-start | bytes 2097152 | tf_op jit(solution)/shard_map/all_to_all | solution.py:145
  537.3 16.6 %collective-permute-start = (bf16[512,512]{1,0:T(8,128)(2,1)}, bf16[512,512]{1,0:T(8,128)(2,1)}, u32[]{:S(2)}, u32[]{:S(2)}) collective-permute-start(bf16[512,512]{1,0:T(8,128)(2,1)} %get-tuple-element.10), channel_id=1, source_target_pairs={{0,1},{1,2},{2,3},{3,0},{4,5},{5,6},{6,7},{7,4},{8,9},{9,10},{10,1... | collective-permute-start | bytes 1572872 | tf_op jit(solution)/shard_map/ppermute | solution.py:23
  539.6 17.3 %collective-permute-start.1 = (bf16[512,512]{1,0:T(8,128)(2,1)}, bf16[512,512]{1,0:T(8,128)(2,1)}, u32[]{:S(2)}, u32[]{:S(2)}) collective-permute-start(bf16[512,512]{1,0:T(8,128)(2,1)} %get-tuple-element.10), channel_id=1, source_target_pairs={{0,3},{1,0},{2,1},{3,2},{4,7},{5,4},{6,5},{7,6},{8,11},{9,8},{10,9... | collective-permute-start | bytes 1572872 | tf_op jit(solution)/shard_map/ppermute | solution.py:26
  553.9 15.6 %collective-permute-start.2 = (bf16[512,512]{1,0:T(8,128)(2,1)}, bf16[512,512]{1,0:T(8,128)(2,1)}, u32[]{:S(2)}, u32[]{:S(2)}) collective-permute-start(bf16[512,512]{1,0:T(8,128)(2,1)} %collective-permute-done), channel_id=1, source_target_pairs={{0,1},{1,2},{2,3},{3,0},{4,5},{5,6},{6,7},{7,4},{8,9},{9,10},{10,1... | collective-permute-start | bytes 1572872 | tf_op jit(solution)/shard_map/ppermute | solution.py:23
  571.3 25.9 %copy-start.3 = (f32[128,1,2048]{2,1,0:T(1,128)S(1)}, f32[128,1,2048]{2,1,0:T(1,128)}, u32[]{:S(2)}) copy-start(f32[128,1,2048]{2,1,0:T(1,128)} %copy-done.2) | copy-start | bytes 3145732
  590.3 40.1 %all-to-all-start.1 = ((f32[128,2,512]{2,1,0:T(2,128)}), f32[128,2,512]{2,1,0:T(2,128)}, u32[]{:S(2)}, u32[]{:S(2)}) async-start(f32[128,2,512]{2,1,0:T(2,128)} %copy.16), calls=%async_computation.1 | async-start | bytes 1048576 | tf_op jit(solution)/shard_map/all_to_all | solution.py:115
  630.4 62.0 %all-to-all-start.6 = ((f32[128,1,2048]{2,1,0:T(1,128)}), f32[128,1,2048]{2,1,0:T(1,128)S(1)}, u32[]{:S(2)}, u32[]{:S(2)}) async-start(f32[128,1,2048]{2,1,0:T(1,128)} %copy.22), calls=%async_computation.7 | async-start | bytes 2097152 | tf_op jit(solution)/shard_map/all_to_all | solution.py:155
  692.4 62.1 %all-to-all-start.8 = ((f32[128,1,2048]{2,1,0:T(1,128)}), f32[128,1,2048]{2,1,0:T(1,128)S(1)}, u32[]{:S(2)}, u32[]{:S(2)}) async-start(f32[128,1,2048]{2,1,0:T(1,128)} %copy.24), calls=%async_computation.9 | async-start | bytes 2097152 | tf_op jit(solution)/shard_map/all_to_all | solution.py:156
Sparse Core Ops, SparseCore 0:
  120.9 45.3 reduce-scatter.1
  321.5 51.0 all-reduce.2
  381.3 62.1 all-reduce.4
